TPU v7x, 128 devices: a whole 4x4x4 slice. The times are simulated.
128 devices in a mesh: tseg: 2 (over y_lo), inp: 64 (over x, z, y_hi, core).
Axes of the slice: x: 4, y: 4 (y_hi: 2, y_lo: 2; y = y_hi * 2 + y_lo), z: 4, core: 2. Of those that a mesh axis runs over, the one named last changes fastest.
Arguments:
- samples: bfloat16 [512, 524288], P('inp', 'tseg')
- delays: int32 [512], P('inp'), may hold values from 0 to 8192, as said below
- flags: int32 [512], P('inp'), may hold values 0 or 1
- taps: float32 [16, 1024], replicated, may hold values from -1.5 to 1.5
Outputs:
- vis_real: float32 [512, 512, 512], P(('tseg', 'inp'))
- vis_imag: float32 [512, 512, 512], P(('tseg', 'inp'))
Inputs may be any that keep to these rules, and one draw needn't show every extreme that they name: `delays`: some input has delay 0 and some input has delay 8192.
All inputs are finite; a program needn't handle non-finite values. No bound on the sum of `flags` on one device may be relied on, other than what follows from the above.
Results may differ from a plain program's by a relative error of at most 0.0075.
Values may be sent and summed in bfloat16 or wider, within the bound.
A program may use at most 64 MiB of HBM per device.

v0:
```python
import functools
import math

import jax
import jax.numpy as jnp
import ml_dtypes
import numpy as np
from jax import lax
from jax.experimental import pallas as pl
from jax.experimental.pallas import tpu as pltpu
from jax.sharding import PartitionSpec as P

MESH = pl.DeviceIdType.MESH
TAPS = 16
FRAME = 1024
HALO = 23552
LANES = 128
BLOCKS = FRAME // LANES
HERE = 8
S_DEV = 256
HALF = 128
CHAN = 4
ROWS = CHAN * 2 * HERE
FIRST = HALO // FRAME + 1
RUN = FIRST + S_DEV + 1
WINDOW = HALF + TAPS
SPLIT = 103
O_STRIDE = HERE + 1
SHAPES = {64: (4, 4, 2), 4: (2, 1, 1)}


def dft_rows(nx, ny, nz):
    count = nx * ny * nz * 2
    inp = count // 2
    k = np.arange(FRAME)[None, :]
    q = np.arange(count * CHAN)[:, None]
    phase = ((q * k) % FRAME).astype(np.float64) * (2.0 * math.pi / FRAME)
    parts = np.stack([np.cos(phase), -np.sin(phase)], axis=1) / math.sqrt(FRAME)
    parts = parts.astype(np.float32).astype(ml_dtypes.bfloat16)
    parts = parts.reshape(2, nx, nz, ny // 2, 2, CHAN * 2, FRAME)
    parts = parts.transpose(1, 3, 0, 2, 4, 5, 6)
    assert inp * 2 == count
    return parts.reshape(nx * ny * nz, 2 * CHAN * 2, FRAME)


class Work:
    def __init__(self, dims, delays, flags, refs):
        self.dims = dims
        self.delays, self.flags = delays, flags
        self.rows_table, self.runs, self.tap_rows, self.delayed, self.frames, self.turned = refs
        nx, ny, nz = dims
        self.inp = nx * nz * ny
        self.tseg = lax.axis_index("tseg")
        self.here = lax.axis_index("inp")
        self.me = self.tseg * self.inp + self.here
        self.my_core = self.here % 2
        self.my_y = ((self.here // 2) % (ny // 2)) * 2 + self.tseg
        self.my_z = (self.here // ny) % nz
        self.my_x = self.here // (ny * nz)
        self.lane = lax.broadcasted_iota(jnp.int32, (HERE, LANES), 1)

    def offset(self, group, step):
        nx, ny, nz = self.dims
        dx = step % nx
        dy = step // nx
        dz = (group + 2 * nz + 2 * nx + 2 * ny - dx - dy) % nz
        return dx, dy, dz

    def chip_at(self, dx, dy, dz):
        nx, ny, nz = self.dims
        return (self.my_x + dx) % nx, (self.my_y + dy) % ny, (self.my_z + dz) % nz

    def chip_of(self, group, step):
        return self.chip_at(*self.offset(group, step))

    def device(self, chip, core):
        nx, ny, nz = self.dims
        x, y, z = chip
        return y % 2, ((x * nz + z) * (ny // 2) + y // 2) * 2 + core

    def tied(self, group, step):
        dx, dy, dz = self.offset(group, step)
        return jnp.logical_or(jnp.logical_or(dx == 2, dy == 2), dz == 2)

    def fetch_table(self, table, sem):
        nx, ny, nz = self.dims
        per_group = nx * ny

        @pl.loop(0, nz * per_group)
        def _(step):
            x, y, z = self.chip_of(step // per_group, step % per_group)
            pltpu.make_async_copy(
                table.at[(x * ny + y) * nz + z],
                self.rows_table.at[step // per_group, step % per_group],
                sem,
            ).start()

    def place_taps(self, taps):
        for block in range(BLOCKS):
            for p in range(TAPS):
                self.tap_rows[pl.ds((block * TAPS + p) * 8, 8), :] = jnp.broadcast_to(
                    taps[p : p + 1, block * LANES : (block + 1) * LANES], (8, LANES)
                )

    def spread(self, source, first, frame_range, unroll):
        row = lax.broadcasted_iota(jnp.int32, (HERE, LANES), 0)
        turn = jnp.zeros((HERE, LANES), jnp.int32)
        for i in range(HERE):
            turn = jnp.where(row == i, self.delays[i] % LANES, turn)
        index = (self.lane - turn + LANES) % LANES

        @pl.loop(*frame_range, unroll=unroll)
        def _(frame):
            values = source[:, pl.ds(pl.multiple_of(frame * FRAME, FRAME), FRAME)].astype(
                jnp.float32
            )
            for block in range(BLOCKS):
                moved = jnp.take_along_axis(
                    values[:, block * LANES : (block + 1) * LANES], index, axis=1
                )
                self.runs[pl.ds(block * HERE * RUN + first + frame, HERE, stride=RUN), :] = moved

    def run_half(self, half):
        base = half * HALF - (TAPS - 1)

        @pl.loop(0, HERE * BLOCKS)
        def _(run):
            i = run // BLOCKS
            block = run % BLOCKS
            delay = self.delays[i]
            keep = self.lane >= delay % LANES
            weight = self.flags[i].astype(jnp.float32)

            def start(back):
                moved = block - delay // LANES - back + 9 * BLOCKS
                return (moved % BLOCKS * HERE + i) * RUN + moved // BLOCKS - 9 + FIRST + base

            now, before = start(0), start(1)
            for f in range(0, WINDOW, 8):
                self.delayed[pl.ds(pl.multiple_of(run * WINDOW, 8) + f, 8), :] = jnp.where(
                    keep, self.runs[pl.ds(now + f, 8), :], self.runs[pl.ds(before + f, 8), :]
                )
            tap = [self.tap_rows[pl.ds((block * TAPS + p) * 8, 8), :] for p in range(TAPS)]
            total = {}
            for f in range(HALF + 8):
                values = self.delayed[pl.ds(run * WINDOW + f, 8), :]
                for p in (f % 8 + 8, f % 8):
                    s = f - p
                    if 0 <= s < HALF:
                        total[s] = tap[p] * values if p == 0 else total[s] + tap[p] * values
                if f % 16 == 15 and f > 16:
                    pair = [total.pop(f - 31), total.pop(f - 23)]
                    self.frames[
                        pl.ds(pl.multiple_of(i * HALF, HALF) + f - 31, 16),
                        pl.ds(pl.multiple_of(block * LANES, LANES), LANES),
                    ] = (jnp.concatenate(pair, axis=0) * weight).astype(jnp.bfloat16)
            pair = [total.pop(HALF - 16), total.pop(HALF - 8)]
            self.frames[
                pl.ds(pl.multiple_of(i * HALF, HALF) + HALF - 16, 16),
                pl.ds(pl.multiple_of(block * LANES, LANES), LANES),
            ] = (jnp.concatenate(pair, axis=0) * weight).astype(jnp.bfloat16)
            assert not total

    def transform(self, group):
        nx, ny, nz = self.dims
        per_group = nx * ny
        rows = self.rows_table[group].reshape(per_group * 16, FRAME)

        for pair in range(HERE // 2):
            values = self.frames[pair * 2 * HALF : (pair + 1) * 2 * HALF, :]
            spectra = lax.dot_general(
                rows, values, (((1,), (1,)), ((), ())), preferred_element_type=jnp.float32
            )
            for dest in range(2 * per_group):
                for j in range(2):
                    self.turned[
                        pl.ds(dest * 8 * O_STRIDE + pair * 2 + j, 8, stride=O_STRIDE), :
                    ] = spectra[dest * 8 : (dest + 1) * 8, j * HALF : (j + 1) * HALF]

    def pack(self, dest, target):
        for m in range(0, 8, 2):
            pair_rows = jnp.concatenate(
                [
                    self.turned[pl.ds((dest * 8 + m) * O_STRIDE, HERE), :],
                    self.turned[pl.ds((dest * 8 + m + 1) * O_STRIDE, HERE), :],
                ],
                axis=0,
            )
            target[m * 8 : (m + 2) * 8, :] = pair_rows.astype(jnp.bfloat16)

    def send(self, source, target, device, send_sem, recv_sem):
        pltpu.make_async_remote_copy(
            src_ref=source,
            dst_ref=target,
            send_sem=send_sem,
            recv_sem=recv_sem,
            device_id=device,
            device_id_type=MESH,
        ).start()

    def pass_by(self, group, step, change, source, relay, send_sem, relay_sem):
        way = (1, 3)[change]
        chip = self.chip_at(*[jnp.where(d == 2, way, 0) for d in self.offset(group, step)])
        slot = (group * self.dims[0] * self.dims[1] + step) * 2
        self.send(
            source.at[slot + (self.my_core + change) % 2],
            relay.at[slot + change],
            self.device(chip, self.my_core),
            send_sem,
            relay_sem.at[slot + change],
        )

    def pass_on(self, group, step, change, relay, relay_sem, target, send_sem, recv_sem):
        way = (1, 3)[change]
        offset = self.offset(group, step)
        slot = (group * self.dims[0] * self.dims[1] + step) * 2 + change
        message = relay.at[slot]
        pltpu.make_async_copy(message, message, relay_sem.at[slot]).wait()
        origin_y, origin_inp = self.device(
            self.chip_at(*[jnp.where(d == 2, 4 - way, 0) for d in offset]), self.my_core
        )
        chip = self.chip_at(*[jnp.where(d == 2, way, d) for d in offset])
        self.send(
            message,
            target.at[origin_y * self.inp + origin_inp],
            self.device(chip, (self.my_core + change) % 2),
            send_sem,
            recv_sem,
        )

    def send_direct(self, group, step, change, source, target, send_sem, recv_sem):
        core = (self.my_core + change) % 2
        slot = (group * self.dims[0] * self.dims[1] + step) * 2 + core
        chip = self.chip_of(group, step)
        self.send(
            source.at[slot], target.at[self.me], self.device(chip, core), send_sem, recv_sem
        )


def exchange_kernel(dims, samples, delays, flags, taps, table, out, raw, rim, ready, *rest):
    relay, refs, sems = rest[0], rest[1:7], rest[7:]
    load_sem, table_sem, rim_send, rim_recv, send_sem, recv_sem, own_sem = sems[:7]
    relay_send, relay_sem = sems[7:]
    work = Work(dims, delays, flags, refs)
    nx, ny, nz = dims
    per_group = nx * ny
    inp = nx * ny * nz
    devices = 2 * inp
    ties = 2 * (inp - (nx - 1) * (ny - 1) * (nz - 1))

    def load(first, count, sem):
        part = pl.ds(first * FRAME, count * FRAME)
        copy = pltpu.make_async_copy(samples.at[:, part], raw.at[:, part], sem)
        copy.start()
        return copy

    late_load = load(SPLIT, S_DEV - SPLIT, load_sem.at[0])
    early_load = load(0, SPLIT, load_sem.at[1])
    barrier = pltpu.get_barrier_semaphore()

    @pl.loop(1, devices)
    def _(step):
        other = (work.me + step) % devices
        pl.semaphore_signal(
            barrier, inc=1, device_id=(other // inp, other % inp), device_id_type=MESH
        )

    work.fetch_table(table, table_sem)
    work.place_taps(taps)

    def pass_by(half, group, step):
        @pl.when(work.tied(group, step))
        def _():
            for change in range(2):
                work.pass_by(
                    group,
                    step,
                    change,
                    ready.at[half],
                    relay.at[half],
                    send_sem.at[half],
                    relay_sem.at[half],
                )

    def pass_on(half, group, step):
        @pl.when(work.tied(group, step))
        def _():
            for change in range(2):
                work.pass_on(
                    group,
                    step,
                    change,
                    relay.at[half],
                    relay_sem.at[half],
                    out.at[half],
                    relay_send.at[half],
                    recv_sem.at[half],
                )

    def send_direct(half, group, step):
        common = (ready.at[half], out.at[half], send_sem.at[half], recv_sem.at[half])

        @pl.when(group + step > 0)
        def _():
            work.send_direct(group, step, 0, *common)

        @pl.when(group + step == 0)
        def _():
            pltpu.make_async_copy(
                ready.at[half, work.my_core], out.at[half, work.me], own_sem.at[half]
            ).start()

        work.send_direct(group, step, 1, *common)

    def transform_half(half):
        @pl.loop(0, nz)
        def _(group):
            work.transform(group)

            @pl.loop(0, per_group, step=4)
            def _(chips):
                for dest in range(8):
                    dest = chips * 2 + dest
                    work.pack(dest, ready.at[half, group * 2 * per_group + dest])

                @pl.loop(0, 4)
                def _(chip):
                    pass_by(half, group, chips + chip)

                @pl.loop(0, 4)
                def _(chip):
                    step = chips + chip

                    @pl.when(jnp.logical_not(work.tied(group, step)))
                    def _():
                        send_direct(half, group, step)

            if half == 0:

                @pl.loop(0, per_group)
                def _(step):
                    pass_on(1, group, step)

    late_load.wait()
    work.spread(raw, FIRST, (SPLIT, S_DEV - 1), 4)
    work.spread(raw, FIRST, (S_DEV - 1, S_DEV), 1)
    pl.semaphore_wait(barrier, devices - 1)
    rim_copy = pltpu.make_async_remote_copy(
        src_ref=samples.at[:, pl.ds(S_DEV * FRAME - HALO, HALO)],
        dst_ref=rim,
        send_sem=rim_send,
        recv_sem=rim_recv,
        device_id=(1 - work.tseg, work.here),
        device_id_type=MESH,
    )
    rim_copy.start()
    work.run_half(1)
    pltpu.make_async_copy(work.rows_table, work.rows_table, table_sem).wait()
    transform_half(1)

    early_load.wait()
    work.spread(raw, FIRST, (0, SPLIT - 3), 4)
    work.spread(raw, FIRST, (SPLIT - 3, SPLIT), 1)
    rim_copy.wait()

    @pl.when(work.tseg == 0)
    def _():
        rim[...] = jnp.zeros_like(rim)

    work.spread(rim, 1, (0, 20), 4)
    work.spread(rim, 1, (20, HALO // FRAME), 1)
    work.run_half(0)
    transform_half(0)

    @pl.loop(0, nz)
    def _(group):
        @pl.loop(0, per_group)
        def _(step):
            pass_on(0, group, step)

    for half in (1, 0):
        pltpu.make_async_copy(
            ready.at[half, work.my_core], out.at[half, work.me], own_sem.at[half]
        ).wait()
        sent = ready.at[half, pl.ds(0, devices - 1)]
        pltpu.make_async_copy(sent, sent, send_sem.at[half]).wait()
        passed = relay.at[half, pl.ds(0, ties)]
        pltpu.make_async_copy(passed, passed, relay_send.at[half]).wait()
        arrived = out.at[half, pl.ds(0, devices - 1)]
        pltpu.make_async_copy(arrived, arrived, recv_sem.at[half]).wait()


def correlate_kernel(segments, scale, spectra, vis_real, vis_imag):
    sources = spectra.shape[1] // segments
    inputs = sources * HERE
    real, imag = [], []
    for half in range(2):
        for segment in range(segments):
            piece = spectra[half, segment * sources : (segment + 1) * sources].astype(jnp.float32)
            real.append(piece[:, :HERE].reshape(inputs, HALF).astype(jnp.bfloat16))
            imag.append(piece[:, HERE:].reshape(inputs, HALF).astype(jnp.bfloat16))
    real = jnp.concatenate(real, axis=1)
    imag = jnp.concatenate(imag, axis=1)

    def product(a, b):
        return lax.dot_general(a, b, (((1,), (1,)), ((), ())), preferred_element_type=jnp.float32)

    middle = inputs // 2
    low, high = slice(0, middle), slice(middle, inputs)
    for rows, columns in ((low, low), (high, high), (low, high)):
        block = product(real[rows], real[columns]) + product(imag[rows], imag[columns])
        vis_real[0, rows, columns] = block * scale
        if rows != columns:
            vis_real[0, columns, rows] = block.T * scale
    cross = product(real, imag)
    vis_imag[0] = (cross - cross.T) * scale


def per_device(samples, delays, flags, taps, *, segments, inp):
    nx, nz, ny_hi = SHAPES[inp]
    dims = (nx, 2 * ny_hi, nz)
    devices = segments * inp
    per_group = nx * 2 * ny_hi
    table = jnp.asarray(dft_rows(*dims))
    anywhere = pl.BlockSpec(memory_space=pl.ANY)
    in_specs = [
        anywhere,
        pl.BlockSpec(memory_space=pltpu.SMEM),
        pl.BlockSpec(memory_space=pltpu.SMEM),
        pl.BlockSpec(memory_space=pltpu.VMEM),
        anywhere,
    ]
    work_scratch = [
        pltpu.VMEM((nz, per_group, 16, FRAME), jnp.bfloat16),
        pltpu.VMEM((BLOCKS * HERE * RUN + 8, LANES), jnp.float32),
        pltpu.VMEM((BLOCKS * TAPS * 8, LANES), jnp.float32),
        pltpu.VMEM((HERE * BLOCKS * WINDOW, LANES), jnp.float32),
        pltpu.VMEM((HERE * HALF, FRAME), jnp.bfloat16),
        pltpu.VMEM((2 * per_group * 8 * O_STRIDE, LANES), jnp.float32),
    ]
    raw = pltpu.VMEM((HERE, S_DEV * FRAME), jnp.bfloat16)
    dma = pltpu.SemaphoreType.DMA
    spectra = pl.pallas_call(
        functools.partial(exchange_kernel, dims),
        out_shape=jax.ShapeDtypeStruct((2, devices, ROWS, HALF), jnp.bfloat16),
        in_specs=in_specs,
        out_specs=anywhere,
        scratch_shapes=[
            raw,
            pltpu.VMEM((HERE, HALO), jnp.bfloat16),
            pltpu.VMEM((2, devices, ROWS, HALF), jnp.bfloat16),
            pltpu.VMEM((2, devices, ROWS, HALF), jnp.bfloat16),
            *work_scratch,
            dma((2,)),
            *[dma] * 3,
            *[dma((2,))] * 4,
            dma((2, devices)),
        ],
        compiler_params=pltpu.CompilerParams(
            collective_id=0, has_side_effects=True, vmem_limit_bytes=60 * 2**20
        ),
        name="exchange",
    )(samples, delays, flags, taps, table)
    inputs = inp * HERE
    visibility = jax.ShapeDtypeStruct((CHAN, inputs, inputs), jnp.float32)
    return pl.pallas_call(
        functools.partial(correlate_kernel, segments, 1.0 / (S_DEV * segments)),
        out_shape=(visibility, visibility),
        grid=(CHAN,),
        in_specs=[pl.BlockSpec((2, devices, 2 * HERE, HALF), lambda c: (0, 0, c, 0))],
        out_specs=(
            pl.BlockSpec((1, inputs, inputs), lambda c: (c, 0, 0)),
            pl.BlockSpec((1, inputs, inputs), lambda c: (c, 0, 0)),
        ),
        compiler_params=pltpu.CompilerParams(vmem_limit_bytes=60 * 2**20),
        name="correlate",
    )(spectra)


def solution(mesh):
    segments, inp = mesh.shape["tseg"], mesh.shape["inp"]
    return jax.shard_map(
        functools.partial(per_device, segments=segments, inp=inp),
        mesh=mesh,
        in_specs=(P("inp", "tseg"), P("inp"), P("inp"), P()),
        out_specs=(P(("tseg", "inp"), None, None), P(("tseg", "inp"), None, None)),
        check_vma=False,
    )
```

profile of v0, /device:TPU:1, one launch (start us, length us, event | category | flops | bytes accessed | tf_op | source)
XLA Modules:
  0.0 90.2 jit_solution(13452549232911897976)
XLA Ops:
  0.6 82.1 %exchange.1.spectra = bf16[2,128,64,128]{3,2,1,0:T(8,128)(2,1)} custom-call(bf16[8,262144]{1,0:T(8,128)(2,1)} %samples.1, s32[8]{0:T(128)} %delays.1, s32[8]{0:T(128)} %flags.1, f32[16,1024]{1,0:T(8,128)} %taps.1, bf16[64,16,1024]{2,1,0:T(8,128)(2,1)} %constant.2.clone.table), custom_call_target="tpu_custom_call" | custom-call | tf_op jit(solution)/shard_map/exchange/pallas_call | solution.py:443
  82.7 7.5 %correlate.1 = (f32[4,512,512]{2,1,0:T(8,128)}, f32[4,512,512]{2,1,0:T(8,128)}) custom-call(bf16[2,128,64,128]{3,2,1,0:T(8,128)(2,1)} %exchange.1.spectra), custom_call_target="tpu_custom_call" | custom-call | tf_op jit(solution)/shard_map/correlate/pallas_call | solution.py:466
where the time goes:
time: 90.9 us; the launch traced here: 90.2 us
  Pallas kernels  89.5 us (98%)
    pallas_call x1, Pallas kernels, per_device(): pl.pallas_call(functools.partial(exchange_kernel, dims), out_shape=jax.Sh...  82.1 us
    pallas_call x1, Pallas kernels, per_device(): pl.pallas_call(functools.partial(correlate_kernel, segments, 1.0 / (S_DEV...  7.46 us

commit v1 on v0

--- a/solution.py
+++ b/solution.py
@@ -62,9 +62,7 @@
     def offset(self, group, step):
         nx, ny, nz = self.dims
         dx = step % nx
-        dy = step // nx
-        dz = (group + 2 * nz + 2 * nx + 2 * ny - dx - dy) % nz
-        return dx, dy, dz
+        return dx, (dx + step // nx) % ny, (dx + group) % nz
 
     def chip_at(self, dx, dy, dz):
         nx, ny, nz = self.dims

time: 90.9 us -> 93.6 us (1.030)
  Pallas kernels: 89.5 us -> 92.7 us
    pallas_call x1, Pallas kernels: 82.1 us -> 85.2 us  [per_device(): pl.pallas_call(functools.partial(exchange_kernel, dims), out_shape=jax.Sh...]
where the time goes in v1:
time: 93.6 us; the launch traced here: 93.3 us
  Pallas kernels  92.7 us (99%)
    pallas_call x1, Pallas kernels, per_device(): pl.pallas_call(functools.partial(exchange_kernel, dims), out_shape=jax.Sh...  85.2 us
    pallas_call x1, Pallas kernels, per_device(): pl.pallas_call(functools.partial(correlate_kernel, segments, 1.0 / (S_DEV...  7.46 us

profile of v1, /device:TPU:1, one launch (start us, length us, event | category | flops | bytes accessed | tf_op | source)
XLA Modules:
  0.0 93.3 jit_solution(16903952204603626968)
XLA Ops:
  0.6 85.2 %exchange.1.spectra = bf16[2,128,64,128]{3,2,1,0:T(8,128)(2,1)} custom-call(bf16[8,262144]{1,0:T(8,128)(2,1)} %samples.1, s32[8]{0:T(128)} %delays.1, s32[8]{0:T(128)} %flags.1, f32[16,1024]{1,0:T(8,128)} %taps.1, bf16[64,16,1024]{2,1,0:T(8,128)(2,1)} %constant.2.clone.table), custom_call_target="tpu_custom_call" | custom-call | tf_op jit(solution)/shard_map/exchange/pallas_call | solution.py:441
  85.8 7.5 %correlate.1 = (f32[4,512,512]{2,1,0:T(8,128)}, f32[4,512,512]{2,1,0:T(8,128)}) custom-call(bf16[2,128,64,128]{3,2,1,0:T(8,128)(2,1)} %exchange.1.spectra), custom_call_target="tpu_custom_call" | custom-call | tf_op jit(solution)/shard_map/correlate/pallas_call | solution.py:464
